TPU v7x, 32 devices: a whole 2x2x4 slice. The times are simulated.
32 devices in a mesh: graph: 16 (over z, x, core), basis: 2 (over y).
Axes of the slice: x: 2, y: 2, z: 4, core: 2. Of those that a mesh axis runs over, the one named last changes fastest.
Arguments:
- edge_feats: bfloat16 [16384, 512], P(('graph', 'basis')), may hold values from -6 to 6
- pre_weight: bfloat16 [512, 512], replicated, may hold values from -0.25 to 0.25
- down_weight: bfloat16 [512, 64], replicated, may hold values from -0.25 to 0.25
- angle_tiles: bfloat16 [384, 2, 128, 128], P('graph', 'basis'), may hold values from -0.5 to 0.5
- part_source: int32 [384], P('graph'), may hold values from 0 to 7
- part_owner: int32 [384, 1], P('graph'), may hold values from 0 to 15; in each aligned block of 24 rows (0 to 23, 24 to 47, ...) at most 3 rows name the same one
- part_target: int32 [384], P('graph'), may hold values from 0 to 7
- up_weight: bfloat16 [2, 64, 512], P('basis'), may hold values from -0.5 to 0.5
- res_first: bfloat16 [512, 512], replicated, may hold values from -0.25 to 0.25
- res_second: bfloat16 [512, 512], replicated, may hold values from -0.25 to 0.25
- edge_slot: int32 [32, 512], P(('graph', 'basis')), may hold values from 0 to 127, never falling along the last dimension, each value on 1 to 8 neighbouring positions
- slot_owner: int32 [32, 128, 1], P(('graph', 'basis')), may hold values from 0 to 15; in each aligned block of 128 rows (0 to 127, 128 to 255, ..., all dimensions but the last counted through in order) at most 16 rows name the same one
- slot_atom: int32 [32, 128], P(('graph', 'basis')), may hold values from 0 to 31
- atom_feats: bfloat16 [1024, 512], P(('graph', 'basis')), may hold values from -6 to 6
- atom_first: bfloat16 [512, 512], replicated, may hold values from -0.25 to 0.25
- atom_second: bfloat16 [512, 512], replicated, may hold values from -0.25 to 0.25
Outputs:
- edge_update: bfloat16 [16384, 512], P(('graph', 'basis'))
- atom_update: bfloat16 [1024, 512], P(('graph', 'basis'))
Inputs may be any that keep to these rules, and one draw needn't show every extreme that they name: `part_owner`: the 24 parts of one graph shard name each shard at most 3 times, a bound that some block reaches. `slot_owner`: the 128 slots of one device name each graph shard at most 16 times, a bound that some block reaches. `edge_slot`: along a device's 512 rows the slot never falls; every slot holds 1 to 8 rows, one exactly 8.
All inputs are finite; a program needn't handle non-finite values.
Results may differ from a plain program's by a relative error of at most 0.015.
Values may be sent and summed in bfloat16 or wider, within the bound.
A program may use at most 64 MiB of HBM per device.

v0:
```python
import functools

import jax
import jax.numpy as jnp
from jax import lax
from jax.experimental import pallas as pl
from jax.experimental.pallas import tpu as pltpu
from jax.sharding import PartitionSpec as P

half_root = 0.5**0.5
MESH = pl.DeviceIdType.MESH
bf16 = jnp.bfloat16
f32 = jnp.float32


def dot(a, b):
    return jnp.dot(a, b, preferred_element_type=f32)


def silu(v):
    return v / (1.0 + jnp.exp(-v))


def lines(shape, axis):
    return lax.broadcasted_iota(jnp.int32, shape, axis)


def far_first(count):
    return sorted(range(1, count), key=lambda k: abs(2 * k - count))


def ranks(row):
    count = row.shape[1]
    down, along = lines((count, count), 0), lines((count, count), 1)
    col = jnp.sum(jnp.where(down == along, row, 0), axis=1, keepdims=True)
    same = jnp.where(col == row, 1, 0)
    rank_row = jnp.sum(jnp.where(down < along, same, 0), axis=0, keepdims=True)
    rank_col = jnp.sum(jnp.where(along < down, same, 0), axis=1, keepdims=True)
    return col, rank_row, rank_col


def kernel(
    n, inner, groups, cap, acap, seat, chunks, nb, block,
    part_source, part_owner, part_target, slot_owner, slot_atom, edge_slot,
    feats_h, pre_h, down_h, angle_h, up_h, first_h, second_h,
    edge_h, gathered,
    edge_out,
    feats, pre, down, angle, up_all, first, second,
    low_all, diag, prod, part_send, part_recv, goals, goals_recv, meta, meta_recv, items_v, items,
    plane_send, plane_recv, paired, pair_recv, pick, atom_send, atom_recv,
    load_sem, item_sem, edge_sem, goal_ss, goal_rs, meta_ss, meta_rs, part_ss, part_rs, plane_ss, plane_rs, atom_ss, atom_rs,
    low_ss, low_rs, up_ss, up_rs, pair_ss, pair_rs,
):
    me = lax.axis_index("graph")
    mine = lax.axis_index("basis")
    outer = n // inner
    layer, spot = me // inner, lax.rem(me, inner)
    half = block // 2
    width = 2 * low_all.shape[3] // 2

    loads = [
        pltpu.make_async_copy(src, dst, load_sem.at[i])
        for i, (src, dst) in enumerate(
            [
                (feats_h, feats), (pre_h, pre), (down_h, down), (angle_h, angle),
                (up_h.at[0], up_all.at[mine]), (first_h, first), (second_h, second),
            ]
        )
    ]
    for load in loads[:3]:
        load.start()

    barrier = pltpu.get_barrier_semaphore()

    def greet(k, carry):
        pl.semaphore_signal(
            barrier, inc=1, device_id=(lax.rem(me + k, n), mine), device_id_type=MESH
        )
        return carry

    lax.fori_loop(1, n, greet, 0)
    for k in range(1, groups):
        pl.semaphore_signal(
            barrier, inc=1, device_id=(me, lax.rem(mine + k, groups)), device_id_type=MESH
        )

    def send(src, dst, ss, rs, to, to_basis):
        return pltpu.make_async_remote_copy(
            src_ref=src, dst_ref=dst, send_sem=ss, recv_sem=rs,
            device_id=(to, to_basis), device_id_type=MESH,
        )

    def meta_copy(d, slot):
        return send(meta.at[d], meta_recv.at[slot], meta_ss.at[d], meta_rs.at[slot], d, mine)

    def goal_copy(q, slot):
        return send(
            goals.at[q], goals_recv.at[slot], goal_ss.at[q], goal_rs.at[slot],
            layer * inner + q, mine,
        )

    def part_copy(h, q, slot):
        return send(
            part_send.at[h, q], part_recv.at[h, slot], part_ss.at[h, q], part_rs.at[h, slot],
            layer * inner + q, mine,
        )

    def plane_copy(h, z, slot):
        return send(
            plane_send.at[h, z], plane_recv.at[h, slot], plane_ss.at[h, z],
            plane_rs.at[h, slot], z * inner + spot, mine,
        )

    def atom_copy(d, slot):
        return send(
            atom_send.at[d], atom_recv.at[slot], atom_ss.at[d], atom_rs.at[slot], d, mine
        )

    def up_copy(g, slot):
        return send(up_h.at[0], up_all.at[slot], up_ss.at[g], up_rs.at[slot], me, g)

    def low_copy(g, slot):
        return send(low_all.at[mine], low_all.at[slot], low_ss.at[g], low_rs.at[slot], me, g)

    def pair_copy(h, g, slot):
        return send(
            paired.at[h, g], pair_recv.at[h, slot], pair_ss.at[h, g], pair_rs.at[h, slot], me, g
        )

    loads[0].wait()
    loads[1].wait()
    for load in loads[3:]:
        load.start()
    projected = silu(dot(feats[...], pre[...])).astype(bf16)
    loads[2].wait()
    down_twice = jnp.concatenate([down[...], down[...]], axis=0)
    lowered = silu(
        lax.dot_general(
            projected, down_twice, (((1,), (1,)), ((), ())), preferred_element_type=f32
        )
    ).reshape(nb, 2, half, width)
    lane = lax.broadcasted_iota(jnp.int32, (nb, half, width), 2)
    low_all[mine] = jnp.where(lane < width // 2, lowered[:, 0], lowered[:, 1]).astype(bf16)

    pl.semaphore_wait(barrier, n - 1 + groups - 1)
    others = [lax.rem(mine + k, groups) for k in range(1, groups)]
    for g in others:
        low_copy(g, mine).start()
    for g in others:
        up_copy(g, mine).start()

    parts = part_owner.shape[1]
    owner = part_owner[...]
    owner = (owner & (inner - 1)) * outer + (owner >> (inner.bit_length() - 1))
    owner_col, rank_row, rank_col = ranks(owner)
    match = lines((n * seat, parts), 0) == owner * seat + rank_row
    goal = jnp.sum(
        jnp.where(match, part_target[...] + 1, 0), axis=1, keepdims=True
    )
    spread_goal = jnp.broadcast_to(goal - 1, (n * seat, 128))
    goals[...] = spread_goal.reshape(inner, outer, seat, 128)
    match = lines((parts, n * seat), 1) == owner_col * seat + rank_col
    items_v[...] = jnp.sum(
        jnp.where(match, lines((parts, n * seat), 0), 0), axis=0, keepdims=True
    )
    item_copy = pltpu.make_async_copy(items_v, items, item_sem.at[0])
    item_copy.start()

    slots = slot_owner.shape[1]
    owner = slot_owner[...]
    owner_col, rank_row, rank_col = ranks(owner)
    match = lines((n * acap, slots), 0) == owner * acap + rank_row
    held = jnp.sum(
        jnp.where(match, lines((n * acap, slots), 1) + 1, 0), axis=1, keepdims=True
    )
    pick[...] = (held - 1 == edge_slot[...]).astype(f32).astype(bf16)
    wanted = jnp.where(
        lines((n, slots), 0) == owner, slot_atom[...].astype(f32) + 1.0, 0.0
    ).astype(bf16)
    first_lane = me * acap
    lanes = (lines((slots, n * acap), 1) == rank_col + first_lane).astype(f32).astype(bf16)
    atom_meta = dot(wanted, lanes).astype(jnp.int32)
    for r in range(chunks):
        meta[:, r, :] = atom_meta[:, r * 128 : (r + 1) * 128]

    spots = [lax.rem(spot + k, inner) for k in far_first(inner)]
    layers = [lax.rem(layer + k, outer) for k in far_first(outer)]
    for q in spots:
        goal_copy(q, spot).start()
    goals_recv[spot] = goals[spot]

    def start_meta(k, carry):
        meta_copy(lax.rem(me + k, n), me).start()
        return carry

    lax.fori_loop(1, n, start_meta, 0)
    meta_recv[me] = meta[me]

    def spread(g):
        lane = lax.broadcasted_iota(jnp.int32, (half, width), 1)
        left = lane < width // 2
        for i in range(nb):
            packed = low_all[g, i].astype(f32)
            turned = pltpu.roll(packed, width // 2, 1)
            at = g * nb + i
            diag[at, 0:half] = jnp.where(left, packed, 0.0).astype(bf16)
            diag[at, half : 2 * half] = jnp.where(left, turned, 0.0).astype(bf16)
            diag[at, 2 * half : 3 * half] = jnp.where(left, 0.0, turned).astype(bf16)
            diag[at, 3 * half :] = jnp.where(left, 0.0, packed).astype(bf16)

    spread(mine)
    loads[3].wait()
    for g in others:
        low_copy(g, g).wait_recv()
        spread(g)

    for p in range(parts):
        tile = angle[p, 0]
        wide = jnp.concatenate([tile[:half], tile[half:]], axis=1)
        prod[p] = dot(wide, diag[part_source[p]]).astype(bf16)
    item_copy.wait()

    pieces = part_send.shape[0]
    piece = half // pieces

    def fill(h, q, ref, slot):
        def fill_layer(z, carry):
            for s in range(cap):
                item = jnp.clip(items[0, (q * outer + z) * seat + s], 0, prod.shape[0] - 1)
                ref[h, slot, z, s] = prod[item, h * piece : (h + 1) * piece]
            return carry

        lax.fori_loop(0, outer, fill_layer, 0)

    for h in range(pieces):
        for q in spots:
            fill(h, q, part_send, q)
            part_copy(h, q, spot).start()
        fill(h, spot, part_recv, spot)

    loads[4].wait()
    for g in others:
        up_copy(g, g).wait_recv()
    blank = jnp.zeros(up_all.shape[1:], bf16)
    above = jnp.concatenate([x for g in range(groups) for x in (up_all[g], blank)], axis=0)
    below = jnp.concatenate([x for g in range(groups) for x in (blank, up_all[g])], axis=0)
    for load in loads[5:]:
        load.wait()

    depth = above.shape[1]
    for q in spots:
        goal_copy(q, q).wait_recv()

    def gather_layer(h):
        for q in spots:
            part_copy(h, q, q).wait_recv()

        def one(z, carry):
            pairs = [
                (goals_recv[q, z, s : s + 1, :], part_recv[h, q, z, s].astype(f32))
                for q in range(inner)
                for s in range(cap)
            ]
            for j in range(groups * nb):
                total = jnp.zeros((piece, width), f32)
                for t, a in pairs:
                    total = total + jnp.where(jnp.broadcast_to(t == j, a.shape), a, 0.0)
                plane_send[h, z, j] = total.astype(bf16)
            return carry

        lax.fori_loop(0, outer, one, 0)
        for z in layers:
            plane_copy(h, z, layer).start()
        plane_recv[h, layer] = plane_send[h, layer]

    def sum_layers(h):
        for z in layers:
            plane_copy(h, z, z).wait_recv()
        total = plane_recv[h, 0].astype(f32)
        for z in range(1, outer):
            total = total + plane_recv[h, z].astype(f32)
        paired[h] = total.astype(bf16).reshape(groups, nb * piece, width)
        for g in others:
            pair_copy(h, g, mine).start()
        pair_recv[h, mine] = paired[h, mine]

    def edge_layers(h):
        for g in others:
            pair_copy(h, g, g).wait_recv()
        columns = jnp.concatenate([pair_recv[h, g] for g in range(groups)], axis=1)
        upper = dot(columns, above).reshape(nb, 1, piece, depth)
        lower = dot(columns, below).reshape(nb, 1, piece, depth)
        triplet = jnp.concatenate([upper, lower], axis=1).reshape(2 * nb * piece, depth)
        starts = [q * half + h * piece for q in range(2 * nb)]
        own = jnp.concatenate([feats[at : at + piece] for at in starts], axis=0)
        joined = (own.astype(f32) + triplet).astype(bf16)
        inner = silu(dot(joined, first[...])).astype(bf16)
        deep = silu(dot(inner, second[...]))
        update = ((joined.astype(f32) + deep) * half_root).astype(bf16)
        for q, at in enumerate(starts):
            edge_out[at : at + piece] = update[q * piece : (q + 1) * piece]

    for h in range(pieces + 3):
        if h < pieces:
            gather_layer(h)
        if 0 <= h - 2 < pieces:
            sum_layers(h - 2)
        if 0 <= h - 3 < pieces:
            edge_layers(h - 3)

    edge_copy = pltpu.make_async_copy(edge_out, edge_h, edge_sem.at[0])
    edge_copy.start()
    atom_send[...] = dot(pick[...], edge_out[...]).astype(bf16).reshape(atom_send.shape)

    def start_atom(i, carry):
        for k in (n // 2 + i, n // 2 - i):
            atom_copy(lax.rem(me + k, n), me).start()
        return carry

    atom_copy(lax.rem(me + n // 2, n), me).start()
    lax.fori_loop(1, n // 2, start_atom, 0)
    atom_recv[me] = atom_send[me]

    def take_meta(i, carry):
        src = lax.rem(me + i, n)
        meta_copy(src, src).wait_recv()
        return carry

    lax.fori_loop(1, n, take_meta, 0)
    named = jnp.sum(meta_recv[...], axis=0)
    atoms = gathered.shape[0]
    ids = lines((atoms, 128), 0) + 1
    chosen = jnp.concatenate(
        [(ids == named[r : r + 1]).astype(f32).astype(bf16) for r in range(chunks)], axis=1
    )

    def take_atom(i, carry):
        src = lax.rem(me + i, n)
        atom_copy(src, src).wait_recv()
        return carry

    lax.fori_loop(1, n, take_atom, 0)
    gathered[...] = dot(
        chosen, atom_recv[...].reshape(n * acap, atom_recv.shape[2])
    ).astype(bf16)
    edge_copy.wait()

    def finish(k, carry):
        d = lax.rem(me + k, n)
        meta_copy(d, me).wait_send()
        atom_copy(d, me).wait_send()
        return carry

    lax.fori_loop(1, n, finish, 0)
    for q in spots:
        goal_copy(q, spot).wait_send()
        for h in range(pieces):
            part_copy(h, q, spot).wait_send()
    for z in layers:
        for h in range(pieces):
            plane_copy(h, z, layer).wait_send()
    for g in others:
        low_copy(g, mine).wait_send()
        up_copy(g, mine).wait_send()
        for h in range(pieces):
            pair_copy(h, g, mine).wait_send()


def atom_layers(
    edge_h, gathered, feats_h, first_h, second_h, edge_out, atom_out,
    edge, feats, first, second, load_sem, in_sem, out_sem,
):
    loads = [
        pltpu.make_async_copy(src, dst, load_sem.at[i])
        for i, (src, dst) in enumerate([(first_h, first), (second_h, second), (feats_h, feats)])
    ]
    share = edge.shape[0] // 4
    strips = [pl.ds(i * share, share) for i in range(4)]
    ins = [
        pltpu.make_async_copy(edge_h.at[at], edge.at[at], in_sem.at[i])
        for i, at in enumerate(strips)
    ]
    outs = [
        pltpu.make_async_copy(edge.at[at], edge_out.at[at], out_sem.at[i])
        for i, at in enumerate(strips)
    ]
    for copy in ins + loads:
        copy.start()
    for arrive, leave in zip(ins, outs):
        arrive.wait()
        leave.start()
    for load in loads:
        load.wait()
    hidden = silu(dot(gathered[...], first[...])).astype(bf16)
    atom_out[...] = (feats[...].astype(f32) + dot(hidden, second[...])).astype(bf16)
    for leave in outs:
        leave.wait()


def body(
    edge_feats, pre_weight, down_weight, angle_tiles, part_source, part_owner, part_target,
    up_weight, res_first, res_second, edge_slot, slot_owner, slot_atom, atom_feats,
    atom_first, atom_second,
):
    n, groups = lax.axis_size("graph"), lax.axis_size("basis")
    parts, _, block, _ = angle_tiles.shape
    narrow = down_weight.shape[1]
    rows, wide = edge_feats.shape
    nb = rows // block
    slot_count = slot_owner.shape[1]
    cap = max(2, 2 * parts // n)
    acap = -(-max(2, 2 * slot_count // n) // 16) * 16

    seat = -(-cap // 8) * 8
    chunks = n * acap // 128
    meta_rows = -(-chunks // 8) * 8
    pieces = min(4, block // 32)
    inner = 1
    while n % (2 * inner) == 0 and inner * inner < n:
        inner *= 2
    outer = n // inner
    piece = block // 2 // pieces

    half, pair_width = block // 2, 2 * narrow
    dma = pltpu.SemaphoreType.DMA
    vmem = pl.BlockSpec(memory_space=pltpu.VMEM)
    hbm = pl.BlockSpec(memory_space=pl.ANY)
    scratch = [
        pltpu.VMEM(edge_feats.shape, bf16),
        pltpu.VMEM(edge_feats.shape, bf16),
        pltpu.VMEM(pre_weight.shape, bf16),
        pltpu.VMEM(down_weight.shape[::-1], bf16),
        pltpu.VMEM(angle_tiles.shape, bf16),
        pltpu.VMEM((groups,) + up_weight.shape[1:], bf16),
        pltpu.VMEM(res_first.shape, bf16),
        pltpu.VMEM(res_second.shape, bf16),
        pltpu.VMEM((groups, nb, half, pair_width), bf16),
        pltpu.VMEM((groups * nb, 2 * block, pair_width), bf16),
        pltpu.VMEM((parts, half, pair_width), bf16),
        pltpu.VMEM((pieces, inner, outer, cap, piece, pair_width), bf16),
        pltpu.VMEM((pieces, inner, outer, cap, piece, pair_width), bf16),
        pltpu.VMEM((inner, outer, seat, 128), jnp.int32),
        pltpu.VMEM((inner, outer, seat, 128), jnp.int32),
        pltpu.VMEM((n, meta_rows, 128), jnp.int32),
        pltpu.VMEM((n, meta_rows, 128), jnp.int32),
        pltpu.VMEM((1, n * seat), jnp.int32),
        pltpu.SMEM((1, n * seat), jnp.int32),
        pltpu.VMEM((pieces, outer, groups * nb, piece, pair_width), bf16),
        pltpu.VMEM((pieces, outer, groups * nb, piece, pair_width), bf16),
        pltpu.VMEM((pieces, groups, nb * piece, pair_width), bf16),
        pltpu.VMEM((pieces, groups, nb * piece, pair_width), bf16),
        pltpu.VMEM((n * acap, rows), bf16),
        pltpu.VMEM((n, acap, wide), bf16),
        pltpu.VMEM((n, acap, wide), bf16),
        dma((7,)),
        dma((1,)),
        dma((1,)),
    ]
    scratch += [dma((inner,))] * 2 + [dma((n,))] * 2 + [dma((pieces, inner))] * 2
    scratch += [dma((pieces, outer))] * 2 + [dma((n,))] * 2
    scratch += [dma((groups,))] * 4 + [dma((pieces, groups))] * 2
    shapes = (
        jax.ShapeDtypeStruct(edge_feats.shape, bf16),
        jax.ShapeDtypeStruct(atom_feats.shape, bf16),
    )
    edge_update, gathered = pl.pallas_call(
        functools.partial(kernel, n, inner, groups, cap, acap, seat, chunks, nb, block),
        out_shape=shapes,
        in_specs=[pl.BlockSpec(memory_space=pltpu.SMEM)] + [vmem] * 5 + [hbm] * 7,
        out_specs=(hbm, vmem),
        scratch_shapes=scratch,
        compiler_params=pltpu.CompilerParams(
            collective_id=0, has_side_effects=True, vmem_limit_bytes=62 * 2**20
        ),
    )(
        part_source, part_owner.reshape(1, parts), part_target.reshape(1, parts),
        slot_owner.reshape(1, slot_count), slot_atom, edge_slot,
        edge_feats, pre_weight, down_weight.T,
        angle_tiles, up_weight, res_first, res_second,
    )
    return pl.pallas_call(
        atom_layers,
        out_shape=shapes,
        in_specs=[hbm, vmem, hbm, hbm, hbm],
        out_specs=(hbm, vmem),
        scratch_shapes=[
            pltpu.VMEM(edge_feats.shape, bf16),
            pltpu.VMEM(atom_feats.shape, bf16),
            pltpu.VMEM(atom_first.shape, bf16),
            pltpu.VMEM(atom_second.shape, bf16),
            dma((3,)),
            dma((4,)),
            dma((4,)),
        ],
        compiler_params=pltpu.CompilerParams(vmem_limit_bytes=62 * 2**20),
    )(edge_update, gathered, atom_feats, atom_first, atom_second)


def solution(mesh):
    rows = P(("graph", "basis"), None)
    in_specs = (
        rows,
        P(),
        P(),
        P("graph", "basis", None, None),
        P("graph"),
        P("graph", None),
        P("graph"),
        P("basis", None, None),
        P(),
        P(),
        rows,
        P(("graph", "basis"), None, None),
        rows,
        rows,
        P(),
        P(),
    )
    return jax.shard_map(
        body, mesh=mesh, in_specs=in_specs, out_specs=(rows, rows), check_vma=False
    )
```

profile of v0, /device:TPU:0, one launch (start us, length us, event | category | flops | bytes accessed | tf_op | source)
XLA Modules:
  0.0 46.2 jit_solution(2924811653547073738)
XLA Ops:
  0.6 42.0 %shard_map.167 = (bf16[512,512]{1,0:T(8,128)(2,1)}, bf16[32,512]{1,0:T(8,128)(2,1)}) custom-call(s32[24]{0:T(128)} %part_source.1, s32[1,24]{1,0:T(1,128)} %bitcast.5, s32[1,24]{1,0:T(1,128)} %bitcast.6, s32[1,128]{1,0:T(1,128)} %bitcast.7, s32[1,128]{1,0:T(1,128)} %slot_atom.1, s32[1,512]{1,0:T(1,128)} %edge_slot.1, bf16[512,512]{1,0:T(8,128)(2,1)} %feats_h.2, ...), custom_call_target="tpu_custom_call" | custom-call | tf_op jit(solution)/shard_map/pallas_call | solution.py:466
  42.7 3.5 %shard_map.168 = (bf16[512,512]{1,0:T(8,128)(2,1)}, bf16[32,512]{1,0:T(8,128)(2,1)}) custom-call(bf16[512,512]{1,0:T(8,128)(2,1)} %get-tuple-element.4.edge_h, bf16[32,512]{1,0:T(8,128)(2,1)} %get-tuple-element.5.gathered, bf16[32,512]{1,0:T(8,128)(2,1)} %feats_h.3, bf16[512,512]{1,0:T(8,128)(2,1)} %first_h.3, bf16[512,512]{1,0:T(8,128)(2,1)} %second_h.3), custom_call_target="tpu_custom_call" | custom-call | tf_op jit(solution)/shard_map/pallas_call | solution.py:481
where the time goes:
time: 46.5 us; the launch traced here: 46.2 us
  Pallas kernels  45.5 us (98%)
  between operations  0.64 us (1%)
    pallas_call x1, Pallas kernels, body(): pl.pallas_call(functools.partial(kernel, n, inner, groups, cap, acap, sea...  42 us
    pallas_call x1, Pallas kernels, body(): pl.pallas_call(atom_layers, out_shape=shapes, in_specs=[hbm, vmem, hbm, h...  3.51 us

commit v1 on v0

--- a/solution.py
+++ b/solution.py
@@ -18,7 +18,8 @@
 
 
 def silu(v):
-    return v / (1.0 + jnp.exp(-v))
+    w = 0.5 * v
+    return w + w * jnp.tanh(w)
 
 
 def lines(shape, axis):
@@ -41,14 +42,15 @@
 
 def kernel(
     n, inner, groups, cap, acap, seat, chunks, nb, block,
-    part_source, part_owner, part_target, slot_owner, slot_atom, edge_slot,
+    source_h, owner_h, target_h, slot_owner_h, slot_atom_h, edge_slot_h,
     feats_h, pre_h, down_h, angle_h, up_h, first_h, second_h,
     edge_h, gathered,
+    part_source, part_owner, part_target, slot_owner, slot_atom, edge_slot,
     edge_out,
     feats, pre, down, angle, up_all, first, second,
     low_all, diag, prod, part_send, part_recv, goals, goals_recv, meta, meta_recv, items_v, items,
     plane_send, plane_recv, paired, pair_recv, pick, atom_send, atom_recv,
-    load_sem, item_sem, edge_sem, goal_ss, goal_rs, meta_ss, meta_rs, part_ss, part_rs, plane_ss, plane_rs, atom_ss, atom_rs,
+    load_sem, small_sem, item_sem, edge_sem, goal_ss, goal_rs, meta_ss, meta_rs, part_ss, part_rs, plane_ss, plane_rs, atom_ss, atom_rs,
     low_ss, low_rs, up_ss, up_rs, pair_ss, pair_rs,
 ):
     me = lax.axis_index("graph")
@@ -67,7 +69,16 @@
             ]
         )
     ]
-    for load in loads[:3]:
+    small = [
+        pltpu.make_async_copy(src, dst, small_sem.at[i])
+        for i, (src, dst) in enumerate(
+            [
+                (source_h, part_source), (owner_h, part_owner), (target_h, part_target),
+                (slot_owner_h, slot_owner), (slot_atom_h, slot_atom), (edge_slot_h, edge_slot),
+            ]
+        )
+    ]
+    for load in loads[:3] + small:
         load.start()
 
     barrier = pltpu.get_barrier_semaphore()
@@ -149,6 +160,8 @@
     for g in others:
         up_copy(g, mine).start()
 
+    for load in small:
+        load.wait()
     parts = part_owner.shape[1]
     owner = part_owner[...]
     owner = (owner & (inner - 1)) * outer + (owner >> (inner.bit_length() - 1))
@@ -166,35 +179,11 @@
     item_copy = pltpu.make_async_copy(items_v, items, item_sem.at[0])
     item_copy.start()
 
-    slots = slot_owner.shape[1]
-    owner = slot_owner[...]
-    owner_col, rank_row, rank_col = ranks(owner)
-    match = lines((n * acap, slots), 0) == owner * acap + rank_row
-    held = jnp.sum(
-        jnp.where(match, lines((n * acap, slots), 1) + 1, 0), axis=1, keepdims=True
-    )
-    pick[...] = (held - 1 == edge_slot[...]).astype(f32).astype(bf16)
-    wanted = jnp.where(
-        lines((n, slots), 0) == owner, slot_atom[...].astype(f32) + 1.0, 0.0
-    ).astype(bf16)
-    first_lane = me * acap
-    lanes = (lines((slots, n * acap), 1) == rank_col + first_lane).astype(f32).astype(bf16)
-    atom_meta = dot(wanted, lanes).astype(jnp.int32)
-    for r in range(chunks):
-        meta[:, r, :] = atom_meta[:, r * 128 : (r + 1) * 128]
-
     spots = [lax.rem(spot + k, inner) for k in far_first(inner)]
     layers = [lax.rem(layer + k, outer) for k in far_first(outer)]
     for q in spots:
         goal_copy(q, spot).start()
     goals_recv[spot] = goals[spot]
-
-    def start_meta(k, carry):
-        meta_copy(lax.rem(me + k, n), me).start()
-        return carry
-
-    lax.fori_loop(1, n, start_meta, 0)
-    meta_recv[me] = meta[me]
 
     def spread(g):
         lane = lax.broadcasted_iota(jnp.int32, (half, width), 1)
@@ -217,7 +206,7 @@
     for p in range(parts):
         tile = angle[p, 0]
         wide = jnp.concatenate([tile[:half], tile[half:]], axis=1)
-        prod[p] = dot(wide, diag[part_source[p]]).astype(bf16)
+        prod[p] = dot(wide, diag[jnp.clip(part_source[p], 0, groups * nb - 1)]).astype(bf16)
     item_copy.wait()
 
     pieces = part_send.shape[0]
@@ -237,6 +226,30 @@
             fill(h, q, part_send, q)
             part_copy(h, q, spot).start()
         fill(h, spot, part_recv, spot)
+
+    slots = slot_owner.shape[1]
+    owner = slot_owner[...]
+    owner_col, rank_row, rank_col = ranks(owner)
+    match = lines((n * acap, slots), 0) == owner * acap + rank_row
+    held = jnp.sum(
+        jnp.where(match, lines((n * acap, slots), 1) + 1, 0), axis=1, keepdims=True
+    )
+    pick[...] = (held - 1 == edge_slot[...]).astype(f32).astype(bf16)
+    wanted = jnp.where(
+        lines((n, slots), 0) == owner, slot_atom[...].astype(f32) + 1.0, 0.0
+    ).astype(bf16)
+    first_lane = me * acap
+    lanes = (lines((slots, n * acap), 1) == rank_col + first_lane).astype(f32).astype(bf16)
+    atom_meta = dot(wanted, lanes).astype(jnp.int32)
+    for r in range(chunks):
+        meta[:, r, :] = atom_meta[:, r * 128 : (r + 1) * 128]
+
+    def start_meta(k, carry):
+        meta_copy(lax.rem(me + k, n), me).start()
+        return carry
+
+    lax.fori_loop(1, n, start_meta, 0)
+    meta_recv[me] = meta[me]
 
     loads[4].wait()
     for g in others:
@@ -367,12 +380,14 @@
 
 
 def atom_layers(
-    edge_h, gathered, feats_h, first_h, second_h, edge_out, atom_out,
-    edge, feats, first, second, load_sem, in_sem, out_sem,
+    edge_h, gathered_h, feats_h, first_h, second_h, edge_out, atom_h,
+    edge, gathered, feats, first, second, atom_out, load_sem, in_sem, out_sem,
 ):
     loads = [
         pltpu.make_async_copy(src, dst, load_sem.at[i])
-        for i, (src, dst) in enumerate([(first_h, first), (second_h, second), (feats_h, feats)])
+        for i, (src, dst) in enumerate(
+            [(gathered_h, gathered), (first_h, first), (second_h, second), (feats_h, feats)]
+        )
     ]
     share = edge.shape[0] // 4
     strips = [pl.ds(i * share, share) for i in range(4)]
@@ -384,7 +399,7 @@
         pltpu.make_async_copy(edge.at[at], edge_out.at[at], out_sem.at[i])
         for i, at in enumerate(strips)
     ]
-    for copy in ins + loads:
+    for copy in loads + ins:
         copy.start()
     for arrive, leave in zip(ins, outs):
         arrive.wait()
@@ -393,6 +408,8 @@
         load.wait()
     hidden = silu(dot(gathered[...], first[...])).astype(bf16)
     atom_out[...] = (feats[...].astype(f32) + dot(hidden, second[...])).astype(bf16)
+    outs.append(pltpu.make_async_copy(atom_out, atom_h, load_sem.at[4]))
+    outs[-1].start()
     for leave in outs:
         leave.wait()
 
@@ -426,6 +443,12 @@
     vmem = pl.BlockSpec(memory_space=pltpu.VMEM)
     hbm = pl.BlockSpec(memory_space=pl.ANY)
     scratch = [
+        pltpu.SMEM((parts,), jnp.int32),
+        pltpu.VMEM((1, parts), jnp.int32),
+        pltpu.VMEM((1, parts), jnp.int32),
+        pltpu.VMEM((1, slot_count), jnp.int32),
+        pltpu.VMEM((1, slot_count), jnp.int32),
+        pltpu.VMEM((1, rows), jnp.int32),
         pltpu.VMEM(edge_feats.shape, bf16),
         pltpu.VMEM(edge_feats.shape, bf16),
         pltpu.VMEM(pre_weight.shape, bf16),
@@ -453,6 +476,7 @@
         pltpu.VMEM((n, acap, wide), bf16),
         pltpu.VMEM((n, acap, wide), bf16),
         dma((7,)),
+        dma((6,)),
         dma((1,)),
         dma((1,)),
     ]
@@ -466,7 +490,7 @@
     edge_update, gathered = pl.pallas_call(
         functools.partial(kernel, n, inner, groups, cap, acap, seat, chunks, nb, block),
         out_shape=shapes,
-        in_specs=[pl.BlockSpec(memory_space=pltpu.SMEM)] + [vmem] * 5 + [hbm] * 7,
+        in_specs=[hbm] * 13,
         out_specs=(hbm, vmem),
         scratch_shapes=scratch,
         compiler_params=pltpu.CompilerParams(
@@ -481,14 +505,16 @@
     return pl.pallas_call(
         atom_layers,
         out_shape=shapes,
-        in_specs=[hbm, vmem, hbm, hbm, hbm],
-        out_specs=(hbm, vmem),
+        in_specs=[hbm] * 5,
+        out_specs=(hbm, hbm),
         scratch_shapes=[
             pltpu.VMEM(edge_feats.shape, bf16),
             pltpu.VMEM(atom_feats.shape, bf16),
+            pltpu.VMEM(atom_feats.shape, bf16),
             pltpu.VMEM(atom_first.shape, bf16),
             pltpu.VMEM(atom_second.shape, bf16),
-            dma((3,)),
+            pltpu.VMEM(atom_feats.shape, bf16),
+            dma((5,)),
             dma((4,)),
             dma((4,)),
         ],

time: 46.5 us -> 44.8 us (0.963)
  Pallas kernels: 45.5 us -> 44 us
    pallas_call x1, Pallas kernels: 3.51 us -> 2.51 us  [body(): pl.pallas_call(atom_layers, out_shape=shapes, in_specs=[hbm] * 5, out_spe...]
    pallas_call x1, Pallas kernels: 42 us -> 41.5 us  [body(): pl.pallas_call(functools.partial(kernel, n, inner, groups, cap, acap, sea...]
where the time goes in v1:
time: 44.8 us; the launch traced here: 44.6 us
  Pallas kernels  44 us (98%)
  between operations  0.64 us (1%)
    pallas_call x1, Pallas kernels, body(): pl.pallas_call(functools.partial(kernel, n, inner, groups, cap, acap, sea...  41.5 us
    pallas_call x1, Pallas kernels, body(): pl.pallas_call(atom_layers, out_shape=shapes, in_specs=[hbm] * 5, out_spe...  2.51 us

profile of v1, /device:TPU:0, one launch (start us, length us, event | category | flops | bytes accessed | tf_op | source)
XLA Modules:
  0.0 44.6 jit_solution(3500849244694211461)
XLA Ops:
  0.6 41.5 %shard_map.167 = (bf16[512,512]{1,0:T(8,128)(2,1)}, bf16[32,512]{1,0:T(8,128)(2,1)}) custom-call(s32[24]{0:T(128)} %source_h.1, s32[1,24]{1,0:T(1,128)} %bitcast.5, s32[1,24]{1,0:T(1,128)} %bitcast.6, s32[1,128]{1,0:T(1,128)} %bitcast.7, s32[1,128]{1,0:T(1,128)} %slot_atom_h.1, s32[1,512]{1,0:T(1,128)} %edge_slot_h.1, bf16[512,512]{1,0:T(8,128)(2,1)} %feats_h.2, ...), custom_call_target="tpu_custom_call" | custom-call | tf_op jit(solution)/shard_map/pallas_call | solution.py:490
  42.1 2.5 %shard_map.168 = (bf16[512,512]{1,0:T(8,128)(2,1)}, bf16[32,512]{1,0:T(8,128)(2,1)}) custom-call(bf16[512,512]{1,0:T(8,128)(2,1)} %get-tuple-element.4.edge_h, bf16[32,512]{1,0:T(8,128)(2,1)} %get-tuple-element.5.gathered_h, bf16[32,512]{1,0:T(8,128)(2,1)} %feats_h.3, bf16[512,512]{1,0:T(8,128)(2,1)} %first_h.3, bf16[512,512]{1,0:T(8,128)(2,1)} %second_h.3), custom_call_target="tpu_custom_call" | custom-call | tf_op jit(solution)/shard_map/pallas_call | solution.py:505
